TPU v7x, 32 devices: a whole 2x2x4 slice. The times are simulated.
32 devices in a mesh: sa: 4 (over y, x), sb: 8 (over z, core).
Axes of the slice: x: 2, y: 2, z: 4, core: 2. Of those that a mesh axis runs over, the one named last changes fastest.
Arguments:
- tokens: bfloat16 [16, 32, 128, 768], P('sa', 'sb'), may hold values from -6 to 6
- cotangent: bfloat16 [16, 32, 128, 768], P('sa', 'sb'), may hold values from -6 to 6
- in_weight: bfloat16 [768, 1536], replicated, may hold values from -0.21875 to 0.21875
- out_weight: bfloat16 [768, 768], replicated, may hold values from -0.21875 to 0.21875
- factor_c: bfloat16 [16, 128, 128], P('sa'), may hold values from -0.5 to 0.5
- factor_a: bfloat16 [32, 16, 16], P('sb'), may hold values from -1.5 to 1.5
- factor_b: bfloat16 [128, 32, 32], P(('sa', 'sb')), may hold values from -1 to 1
Outputs:
- grad_tokens: bfloat16 [16, 32, 128, 768], P('sa', 'sb')
- grad_in_weight: float32 [768, 1536], replicated
- grad_out_weight: float32 [768, 768], replicated
- grad_factor_c: float32 [16, 128, 128], P('sa')
- grad_factor_a: float32 [32, 16, 16], P('sb')
- grad_factor_b: float32 [128, 32, 32], P(('sa', 'sb'))
All inputs are finite; a program needn't handle non-finite values.
Results may differ from a plain program's by a relative error of at most 0.0087.
Values may be sent and summed in bfloat16 or wider, within the bound.
A program may use at most 128 MiB of HBM per device.

v0:
```python
import math

import jax
import jax.numpy as jnp
from jax import lax
from jax.sharding import PartitionSpec as P

CONTRACT_ROWS = (((0,), (0,)), ((), ()))
CONTRACT_COLUMNS = (((1,), (1,)), ((), ()))


def product_rows(left, right):
    return lax.dot_general(left, right, CONTRACT_ROWS, preferred_element_type=jnp.float32)


def product_columns(left, right):
    return lax.dot_general(left, right, CONTRACT_COLUMNS, preferred_element_type=jnp.float32)


def mix_einsum(formula, left, right):
    return jnp.einsum(formula, left, right, preferred_element_type=jnp.float32)


def body(tokens, cotangent, in_weight, out_weight, factor_c, factor_a, factor_b):
    a_dev, b_dev, positions, channels = tokens.shape
    row_count = a_dev * b_dev * positions
    outer_count = lax.axis_size("sa")
    inner_count = lax.axis_size("sb")
    grad_scale = 1.0 / math.sqrt(row_count * outer_count * inner_count)
    flat_tokens = tokens.reshape(row_count, channels)
    projected = jnp.dot(flat_tokens, in_weight, preferred_element_type=jnp.float32)
    queries = projected[:, :channels].astype(jnp.bfloat16)
    values_grid = projected[:, channels:].astype(jnp.bfloat16).reshape(tokens.shape)
    flat_cotangent = cotangent.reshape(row_count, channels)
    query_wide = queries.astype(jnp.float32)
    sigmoid_q = jax.nn.sigmoid(query_wide)
    activation = query_wide * sigmoid_q
    slope = sigmoid_q * (1.0 + query_wide * (1.0 - sigmoid_q))
    grad_gated = product_columns(flat_cotangent, out_weight)
    grad_mixing = (grad_gated * activation).astype(jnp.bfloat16).reshape(tokens.shape)
    section_one = mix_einsum("akc,abcd->abkd", factor_c, values_grid).astype(jnp.bfloat16)
    outer_grid = lax.all_to_all(section_one, "sa", split_axis=2, concat_axis=0, tiled=True)
    section_two = mix_einsum("bka,abcd->kbcd", factor_a, outer_grid).astype(jnp.bfloat16)
    inner_grid = lax.all_to_all(section_two, "sb", split_axis=2, concat_axis=1, tiled=True)
    mixing_inner = mix_einsum("ckb,abcd->akcd", factor_b, inner_grid).astype(jnp.bfloat16)
    mixing_outer = lax.all_to_all(mixing_inner, "sb", split_axis=1, concat_axis=2, tiled=True)
    mixing_grid = lax.all_to_all(mixing_outer, "sa", split_axis=0, concat_axis=2, tiled=True)
    grad_inner = lax.all_to_all(
        lax.all_to_all(grad_mixing, "sa", split_axis=2, concat_axis=0, tiled=True),
        "sb",
        split_axis=2,
        concat_axis=1,
        tiled=True,
    )
    grad_two = mix_einsum("ckb,akcd->abcd", factor_b, grad_inner).astype(jnp.bfloat16)
    grad_fb = mix_einsum("akcd,abcd->ckb", grad_inner, inner_grid)
    grad_two_outer = lax.all_to_all(grad_two, "sb", split_axis=1, concat_axis=2, tiled=True)
    grad_one = mix_einsum("bka,kbcd->abcd", factor_a, grad_two_outer).astype(jnp.bfloat16)
    part_fa = mix_einsum("kbcd,abcd->bka", grad_two_outer, outer_grid)
    grad_one_tokens = lax.all_to_all(grad_one, "sa", split_axis=0, concat_axis=2, tiled=True)
    grad_values_grid = mix_einsum("akc,abkd->abcd", factor_c, grad_one_tokens).astype(jnp.bfloat16)
    part_fc = mix_einsum("abkd,abcd->akc", grad_one_tokens, values_grid)
    grad_fa = lax.psum(part_fa, "sa")
    grad_fc = lax.psum(part_fc, "sb")
    mixing_wide = mixing_grid.reshape(row_count, channels).astype(jnp.float32)
    gated = (activation * mixing_wide).astype(jnp.bfloat16)
    grad_queries = (grad_gated * mixing_wide * slope).astype(jnp.bfloat16)
    grad_queries, part_out = (grad_queries, product_rows(gated, flat_cotangent))
    grad_projected = jnp.concatenate(
        [grad_queries, grad_values_grid.reshape(row_count, channels)], axis=1
    )
    grad_tokens = (
        product_columns(grad_projected, in_weight).astype(jnp.bfloat16).reshape(tokens.shape)
    )
    grad_tokens, part_in = (grad_tokens, product_rows(flat_tokens, grad_projected))
    sum_in, sum_out = lax.psum((part_in, part_out), ("sa", "sb"))
    return (
        grad_tokens,
        sum_in * grad_scale,
        sum_out * grad_scale,
        grad_fc * grad_scale,
        grad_fa * grad_scale,
        grad_fb * grad_scale,
    )


def solution(mesh):
    return jax.shard_map(
        body,
        mesh=mesh,
        in_specs=(
            P("sa", "sb", None, None),
            P("sa", "sb", None, None),
            P(),
            P(),
            P("sa", None, None),
            P("sb", None, None),
            P(("sa", "sb"), None, None),
        ),
        out_specs=(
            P("sa", "sb", None, None),
            P(),
            P(),
            P("sa", None, None),
            P("sb", None, None),
            P(("sa", "sb"), None, None),
        ),
        check_vma=False,
    )
```

profile of v0, /device:TPU:0, one launch (start us, length us, event | category | flops | bytes accessed | tf_op | source)
XLA Modules:
  0.0 809.6 jit_solution(5611380320554375015)
XLA Ops:
  7.2 7.5 convolution_convert_fusion
  14.7 0.2 slice.10
  14.9 2.4 copy-done.7
  17.3 1.6 copy-done.2
  19.0 2.9 convert_bitcast_fusion.5
  21.9 6.2 copy.77
  28.1 41.8 %all_to_all.135 = bf16[4,4,128,768]{3,1,0,2:T(4,128)(2,1)S(1)} all-to-all(bf16[4,4,128,768]{3,1,0,2:T(4,128)(2,1)} %copy.77), channel_id=1, replica_groups=mesh['sa'=4,'sb'=8] {'sa'}, dimensions={2} | all-to-all | bytes 6291456 | tf_op jit(solution)/shard_map/all_to_all | solution.py:42
  69.9 1.0 copy.78
  70.9 4.1 copy.79
  75.0 6.0 all_to_all.101
  81.0 2.8 convert_bitcast_fusion.4
  83.8 0.4 copy.80
  84.2 76.6 %all_to_all.136 = bf16[16,4,32,768]{3,0,1,2:T(8,128)(2,1)S(1)} all-to-all(bf16[16,4,32,768]{3,0,1,2:T(8,128)(2,1)S(1)} %copy.80), channel_id=1, replica_groups=mesh['sa'=4,'sb'=8] {'sb'}, dimensions={2} | all-to-all | bytes 6291456 | tf_op jit(solution)/shard_map/all_to_all | solution.py:44
  160.8 3.3 copy.117
  164.1 6.0 all_to_all.105
  170.1 2.8 convert_bitcast_fusion.3
  172.9 1.7 copy.82
  174.7 74.0 %all_to_all.137 = bf16[16,32,4,768]{3,0,2,1:T(8,128)(2,1)S(1)} all-to-all(bf16[16,32,4,768]{3,0,2,1:T(8,128)(2,1)S(1)} %copy.82), channel_id=1, replica_groups=mesh['sa'=4,'sb'=8] {'sb'}, dimensions={1} | all-to-all | bytes 6291456 | tf_op jit(solution)/shard_map/all_to_all | solution.py:46
  248.7 0.3 copy.83
  249.0 1.0 copy.84
  250.0 39.3 %all_to_all.138 = bf16[16,4,32,768]{3,2,1,0:T(8,128)(2,1)S(1)} all-to-all(bf16[16,4,32,768]{3,2,1,0:T(8,128)(2,1)S(1)} %copy.84), channel_id=1, replica_groups=mesh['sa'=4,'sb'=8] {'sa'}, dimensions={0} | all-to-all | bytes 6291456 | tf_op jit(solution)/shard_map/all_to_all | solution.py:47
  289.3 0.8 convert_bitcast_fusion
  290.2 0.7 copy.85
  291.0 0.6 slice-done
  291.5 0.9 slice-done.1
  292.4 0.3 copy-done.11
  292.7 6.9 fusion.7
  299.6 2.4 copy.86
  302.0 37.8 %all_to_all.139 = bf16[4,4,128,768]{3,1,0,2:T(4,128)(2,1)S(1)} all-to-all(bf16[4,4,128,768]{3,1,0,2:T(4,128)(2,1)S(1)} %copy.86), channel_id=1, replica_groups=mesh['sa'=4,'sb'=8] {'sa'}, dimensions={2} | all-to-all | bytes 6291456 | tf_op jit(solution)/shard_map/all_to_all | solution.py:49
  339.8 1.0 copy.87
  340.8 0.2 copy.88
  341.1 2.4 copy.89
  343.5 75.6 %all_to_all.140 = bf16[16,4,32,768]{3,1,0,2:T(4,128)(2,1)S(1)} all-to-all(bf16[16,4,32,768]{3,1,0,2:T(4,128)(2,1)S(1)} %copy.89), channel_id=1, replica_groups=mesh['sa'=4,'sb'=8] {'sb'}, dimensions={2} | all-to-all | bytes 6291456 | tf_op jit(solution)/shard_map/all_to_all | solution.py:48
  419.1 0.4 copy.90
  419.5 4.1 copy.91
  423.6 5.9 all_to_all.118
  429.5 2.9 convert_bitcast_fusion.2
  432.5 1.7 copy.93
  434.2 74.0 %all_to_all.141 = bf16[16,32,4,768]{3,0,2,1:T(8,128)(2,1)S(1)} all-to-all(bf16[16,32,4,768]{3,0,2,1:T(8,128)(2,1)S(1)} %copy.93), channel_id=1, replica_groups=mesh['sa'=4,'sb'=8] {'sb'}, dimensions={1} | all-to-all | bytes 6291456 | tf_op jit(solution)/shard_map/all_to_all | solution.py:57
  508.2 0.3 copy.94
  508.6 1.0 convert_bitcast_fusion.1
  509.6 0.6 copy-done.4
  510.2 2.7 copy.96
  512.9 4.7 all-to-all-start.7
  517.6 0.2 all-reduce.4.cloned.1.call-start
  517.8 6.0 fusion.21
  523.8 29.9 %all-to-all-done.7 = bf16[16,4,32,768]{3,2,1,0:T(8,128)(2,1)} async-done(((bf16[16,4,32,768]{3,2,1,0:T(8,128)(2,1)}), bf16[16,4,32,768]{3,2,1,0:T(8,128)(2,1)}, u32[]{:S(2)}, u32[]{:S(2)}) %all-to-all-start.7) | async-done | bytes 3145760 | tf_op jit(solution)/shard_map/all_to_all | solution.py:60
  553.7 2.3 copy.97
  556.1 1.7 copy-done.6
  557.7 1.7 convolution_bitcast_fusion
  559.4 4.6 convolution_convert_fusion.1
  564.1 11.1 %fusion.10 = f32[768,1536]{0,1:T(8,128)} fusion(bf16[2048,768]{1,0:T(8,128)(2,1)} %bitcast.148, bf16[2048,768]{1,0:T(8,128)(2,1)} %bitcast.142, bf16[2048,768]{1,0:T(8,128)(2,1)} %get-tuple-element.39), kind=kOutput, calls=%fused_computation.19 | convolution fusion | flops 4844421120 | bytes 14155776 | tf_op jit(solution)/shard_map/dot_general | solution.py:13
  575.2 4.6 fusion.12
  579.8 0.1 copy-done.5
  579.9 1.4 convolution_bitcast_fusion.2
  581.3 15.6 %psum.31 = f32[4,16,16]{2,1,0:T(8,128)S(1)} all-reduce(f32[4,16,16]{2,1,0:T(8,128)S(1)} %convolution_bitcast_fusion.2), channel_id=1, replica_groups=mesh['sa'=4,'sb'=8] {'sa'}, use_global_device_ids=true, to_apply=%region_3.0 | all-reduce | flops 1024 | bytes 8192 | tf_op jit(solution)/shard_map/psum | solution.py:63
  596.9 0.6 broadcast_multiply_fusion.3
  597.5 9.1 %fusion.11 = bf16[2048,768]{1,0:T(8,128)(2,1)} fusion(bf16[768,1536]{1,0:T(8,128)(2,1)} %param.9, bf16[2048,768]{1,0:T(8,128)(2,1)} %bitcast.143, bf16[2048,768]{1,0:T(8,128)(2,1)} %get-tuple-element.39), kind=kOutput, calls=%fused_computation.20 | convolution fusion | flops 4845993984 | bytes 11796480 | tf_op jit(solution)/shard_map/dot_general | solution.py:17
  606.6 11.1 %all-reduce.4.cloned.1.call-done = f32[4,128,128]{2,1,0:T(8,128)} async-done(((f32[4,128,128]{2,1,0:T(8,128)}), f32[4,128,128]{2,1,0:T(8,128)}) %all-reduce.4.cloned.1.call-update) | async-done | bytes 262160 | tf_op jit(solution)/shard_map/psum | solution.py:64
  617.7 1.7 broadcast_multiply_fusion.2
  619.4 169.2 %all-reduce.6.cloned.1.call-done = (f32[768,1536]{0,1:T(8,128)}, f32[768,768]{1,0:T(8,128)}) async-done(((f32[768,1536]{0,1:T(8,128)}, f32[768,768]{1,0:T(8,128)}), (f32[768,1536]{0,1:T(8,128)}, f32[768,768]{1,0:T(8,128)})) %all-reduce.6.cloned.1.call-update) | async-done | bytes 7077904 | tf_op jit(solution)/shard_map/psum | solution.py:76
  788.6 4.8 broadcast_multiply_fusion
  793.3 6.0 copy.99
  799.4 3.2 broadcast_multiply_fusion.1
  (24 shorter events, 0.1 us)
Async XLA Ops:
  7.2 283.8 %copy-start = (bf16[4,4,128,768]{3,2,1,0:T(8,128)(2,1)S(1)}, bf16[4,4,128,768]{3,2,1,0:T(8,128)(2,1)}, u32[]{:S(2)}) copy-start(bf16[4,4,128,768]{3,2,1,0:T(8,128)(2,1)} %param.8) | copy-start | bytes 9437188
  14.7 2.6 copy-start.7
  14.7 4.3 copy-start.8
  17.3 1.6 copy-start.2
  75.0 6.0 copy-start.10
  164.1 6.0 copy-start.9
  289.3 2.2 slice-start
  290.2 2.2 slice-start.1
  290.2 2.5 copy-start.11
  508.5 1.7 copy-start.4
  512.9 40.7 %all-to-all-start.7 = ((bf16[16,4,32,768]{3,2,1,0:T(8,128)(2,1)}), bf16[16,4,32,768]{3,2,1,0:T(8,128)(2,1)}, u32[]{:S(2)}, u32[]{:S(2)}) async-start(bf16[16,4,32,768]{3,2,1,0:T(8,128)(2,1)} %copy.96), calls=%async_computation.7 | async-start | bytes 6291456 | tf_op jit(solution)/shard_map/all_to_all | solution.py:60
  517.6 100.1 %all-reduce.4.cloned.1.call-start = ((), (), s32[]{:S(2)}) async-start(), calls=%async_computation.8 | async-start | bytes 524288 | tf_op jit(solution)/shard_map/psum | solution.py:64
  553.7 4.0 copy-start.3
  556.0 1.7 copy-start.6
  564.0 224.5 %all-reduce.6.cloned.1.call-start = ((), (), s32[]{:S(2)}) async-start(), calls=%async_computation.9 | async-start | bytes 14155776 | tf_op jit(solution)/shard_map/psum | solution.py:76
  575.2 4.6 copy-start.1
  575.2 4.7 copy-start.5
Sparse Core Ops, SparseCore 0:
  564.1 53.5 all-reduce.3
  625.2 163.3 all-reduce.5
where the time goes:
time: 818 us; the launch traced here: 810 us
  blocking collectives  435 us (53%)
  waiting for transfers between devices  210 us (26%)
  local copies, waits for them, and re-layouts  68.9 us (8%)
  matrix products  65.3 us (8%)
  between operations  14.5 us (2%)
  other arithmetic  11.1 us (1%)
    psum x1, waiting for transfers between devices, body(): sum_in, sum_out = lax.psum((part_in, part_out), ('sa', 'sb'))  169 us
    all_to_all x1, blocking collectives, body(): lax.all_to_all(section_two, 'sb', split_axis=2, concat_axis=1, tiled=True)  76.6 us
    all_to_all x1, blocking collectives, body(): lax.all_to_all(lax.all_to_all(grad_mixing, 'sa', split_axis=2, concat_axi...  75.6 us
    all_to_all x1, blocking collectives, body(): lax.all_to_all(mixing_inner, 'sb', split_axis=1, concat_axis=2, tiled=True)  74 us
    all_to_all x1, blocking collectives, body(): lax.all_to_all(grad_two, 'sb', split_axis=1, concat_axis=2, tiled=True)  74 us
    all_to_all x1, blocking collectives, body(): lax.all_to_all(section_one, 'sa', split_axis=2, concat_axis=0, tiled=True)  41.8 us
    all_to_all x1, blocking collectives, body(): lax.all_to_all(mixing_outer, 'sa', split_axis=0, concat_axis=2, tiled=True)  39.3 us
    all_to_all x1, blocking collectives, body(): lax.all_to_all(grad_mixing, 'sa', split_axis=2, concat_axis=0, tiled=True)  37.8 us
  transfers between devices with their start and end apart: 3, of which 3 were waited for; matrix products, arithmetic and copies ran while one was open for 4% of the time, Pallas kernels for 0%

commit v1 on v0

v1 whole, which is shorter than its diff:
```python
import functools
import math

import jax
import jax.numpy as jnp
from jax import lax
from jax.experimental import pallas as pl
from jax.experimental.pallas import tpu as pltpu
from jax.sharding import PartitionSpec as P

CONTRACT_ROWS = (((0,), (0,)), ((), ()))
CONTRACT_COLUMNS = (((1,), (1,)), ((), ()))
S1, B1, B2, S2, S3, B3, B4, S4 = range(8)


def product_rows(left, right):
    return lax.dot_general(left, right, CONTRACT_ROWS, preferred_element_type=jnp.float32)


def product_columns(left, right):
    return lax.dot_general(left, right, CONTRACT_COLUMNS, preferred_element_type=jnp.float32)


def product(left, right):
    return jnp.dot(left, right, preferred_element_type=jnp.float32)


def mixer_kernel(
    dims,
    v_ref, g_ref, fc_ref, perm_ref, ma_ref, mb_ref,
    mix_ref, gv_ref, gfc_ref, gfa_ref, gfb_ref,
    send1, send2, send3, og, ig, mo, mi, go, gi, g2o, g1t,
    send_sem, recv_sem,
):
    na, nb, a_dev, b_dev, positions, rows_c, group, rows_b, width, chunks = dims
    block = a_dev * rows_c
    outer_rows = na * block
    me_a = lax.axis_index("sa")
    me_b = lax.axis_index("sb")
    bf16 = jnp.bfloat16

    def peer_a(t):
        return lax.rem(me_a + t, na)

    def peer_b(t):
        return lax.rem(me_b + t, nb)

    barrier = pltpu.get_barrier_semaphore()

    def greet_a(t, carry):
        pl.semaphore_signal(barrier, inc=1, device_id={"sa": peer_a(t)}, device_id_type=pl.DeviceIdType.MESH)
        return carry

    def greet_b(t, carry):
        pl.semaphore_signal(barrier, inc=1, device_id={"sb": peer_b(t)}, device_id_type=pl.DeviceIdType.MESH)
        return carry

    lax.fori_loop(1, na, greet_a, 0)
    lax.fori_loop(1, nb, greet_b, 0)
    pl.semaphore_wait(barrier, na + nb - 2)

    gfc_ref[...] = jnp.zeros_like(gfc_ref)
    gfa_ref[...] = jnp.zeros_like(gfa_ref)
    gfb_ref[...] = jnp.zeros_like(gfb_ref)

    def scatter_copy(op, q, src, dst, peer, slot):
        return pltpu.make_async_remote_copy(
            src_ref=src.at[q, peer],
            dst_ref=dst.at[q, :, slot],
            send_sem=send_sem.at[op, q, peer],
            recv_sem=recv_sem.at[op, q, slot],
            device_id={"sa": peer},
            device_id_type=pl.DeviceIdType.MESH,
        )

    def collect_copy(op, q, src, dst, peer, slot):
        return pltpu.make_async_remote_copy(
            src_ref=src.at[q, :, peer],
            dst_ref=dst.at[q, slot],
            send_sem=send_sem.at[op, q, peer],
            recv_sem=recv_sem.at[op, q, slot],
            device_id={"sa": peer},
            device_id_type=pl.DeviceIdType.MESH,
        )

    def middle_copy(op, q, src, dst, peer, slot):
        return pltpu.make_async_remote_copy(
            src_ref=src.at[q, :, peer] if op in (B2, B4) else src.at[q, peer],
            dst_ref=dst.at[q, slot],
            send_sem=send_sem.at[op, q, peer],
            recv_sem=recv_sem.at[op, q, slot],
            device_id={"sb": peer},
            device_id_type=pl.DeviceIdType.MESH,
        )

    plan = {
        S1: (scatter_copy, send1, og),
        S2: (collect_copy, mo, mi),
        S3: (scatter_copy, send3, go),
        S4: (collect_copy, send2, g1t),
        B1: (middle_copy, send2, ig),
        B2: (middle_copy, send1, mo),
        B3: (middle_copy, go, gi),
        B4: (middle_copy, send3, g2o),
    }

    def start(op, q):
        make, src, dst = plan[op]
        over_b = make is middle_copy
        me, size, peer_of = (me_b, nb, peer_b) if over_b else (me_a, na, peer_a)

        def one(t, carry):
            make(op, q, src, dst, peer_of(t), me).start()
            return carry

        lax.fori_loop(1, size, one, 0)
        if make is scatter_copy:
            dst[q, :, me] = src[q, me]
        elif op in (B1, B3):
            dst[q, me] = src[q, me]
        else:
            dst[q, me] = src[q, :, me]

    def wait(op, q, sends):
        make, src, dst = plan[op]
        size, peer_of = (nb, peer_b) if make is middle_copy else (na, peer_a)

        def one(t, carry):
            peer = peer_of(t)
            copy = make(op, q, src, dst, peer, peer)
            if sends:
                copy.wait_send()
            else:
                copy.wait_recv()
            return carry

        lax.fori_loop(1, size, one, 0)

    pairs = group * b_dev
    span = pairs * positions
    steps_c = a_dev // group
    slab = group * rows_c

    def columns(q):
        return slice(q * width, (q + 1) * width)

    def native(s, p):
        return pl.ds(pl.multiple_of(s * span + p * positions, 128), positions)

    def slab_rows(s):
        return pl.ds(pl.multiple_of(s * slab, 16), slab)

    def spread(value, dst, q, s):
        moved = product(perm_ref[...], value).astype(bf16)
        dst[q, :, :, slab_rows(s), :] = moved.reshape(na, nb, slab, width)

    def unspread(src, q, s):
        value = src[q, :, :, slab_rows(s), :].reshape(span, width)
        return product_rows(perm_ref[...], value).astype(bf16)

    def stage_c(q):
        def one(s, carry):
            parts = [
                product(fc_ref[s * group + p // b_dev], v_ref[native(s, p), columns(q)]).astype(bf16)
                for p in range(pairs)
            ]
            spread(jnp.concatenate(parts, axis=0), send1, q, s)
            return carry

        lax.fori_loop(0, steps_c, one, 0)
        start(S1, q)

    def stage_g0(q):
        def one(s, carry):
            rows = pl.ds(pl.multiple_of(s * span, 128), span)
            spread(g_ref[rows, columns(q)], send3, q, s)
            return carry

        lax.fori_loop(0, steps_c, one, 0)
        start(S3, q)

    def stage_a(q):
        wait(S1, q, False)

        def one(m, carry):
            value = og[q, m].reshape(outer_rows, width)
            send2[q, m] = product(ma_ref[...], value).astype(bf16).reshape(na, block, width)
            return carry

        lax.fori_loop(0, nb, one, 0)
        start(B1, q)

    def stage_g1(q):
        wait(S3, q, False)
        start(B3, q)

    per_block = block // rows_b

    def middle(ref, q, t):
        rows = pl.ds(pl.multiple_of(lax.rem(t, per_block) * rows_b, 16), rows_b)
        return ref[q, :, lax.div(t, per_block), rows, :].reshape(nb * rows_b, width)

    def put_middle(ref, q, t, value):
        rows = pl.ds(pl.multiple_of(lax.rem(t, per_block) * rows_b, 16), rows_b)
        ref[q, lax.div(t, per_block), :, rows, :] = value.astype(bf16).reshape(nb, rows_b, width)

    def stage_b(q):
        wait(B1, q, False)
        wait(S1, q, True)

        def one(t, carry):
            put_middle(send1, q, t, product(mb_ref[...], middle(ig, q, t)))
            return carry

        lax.fori_loop(0, outer_rows // rows_b, one, 0)
        start(B2, q)

    def stage_g2(q):
        wait(B3, q, False)
        wait(S3, q, True)

        def one(t, carry):
            put_middle(send3, q, t, product_rows(mb_ref[...], middle(gi, q, t)))
            return carry

        lax.fori_loop(0, outer_rows // rows_b, one, 0)
        start(B4, q)

        def gram(t, carry):
            gfb_ref[...] += product_columns(middle(gi, q, t), middle(ig, q, t))
            return carry

        lax.fori_loop(0, outer_rows // rows_b, gram, 0)

    def stage_m1(q):
        wait(B2, q, False)
        start(S2, q)

    def stage_g3(q):
        wait(B4, q, False)
        wait(B1, q, True)

        def one(m, carry):
            grad = g2o[q, m].reshape(outer_rows, width)
            send2[q, m] = product_rows(ma_ref[...], grad).astype(bf16).reshape(na, block, width)
            return carry

        lax.fori_loop(0, nb, one, 0)
        start(S4, q)

        def gram(m, carry):
            gfa_ref[...] += product_columns(
                g2o[q, m].reshape(outer_rows, width), og[q, m].reshape(outer_rows, width)
            )
            return carry

        lax.fori_loop(0, nb, gram, 0)

    def stage_m2(q):
        wait(S2, q, False)

        def one(s, carry):
            rows = pl.ds(pl.multiple_of(s * span, 128), span)
            mix_ref[rows, columns(q)] = unspread(mi, q, s)
            return carry

        lax.fori_loop(0, steps_c, one, 0)

    def stage_g4(q):
        wait(S4, q, False)

        def one(s, carry):
            grad = unspread(g1t, q, s)
            for p in range(pairs):
                part = grad[p * positions : (p + 1) * positions]
                outer = s * group + p // b_dev
                gv_ref[native(s, p), columns(q)] = product_rows(fc_ref[outer], part).astype(bf16)
                gfc_ref[outer] += product_columns(part, v_ref[native(s, p), columns(q)])
            return carry

        lax.fori_loop(0, steps_c, one, 0)

    every = range(chunks)
    for q in every:
        stage_c(q)
    for q in every:
        stage_a(q)
        stage_g0(q)
    for q in every:
        stage_b(q)
        stage_g1(q)
    for q in every:
        stage_g2(q)
        stage_m1(q)
    for q in every:
        stage_m2(q)
    for q in every:
        stage_g3(q)
    for q in every:
        stage_g4(q)
    for q in every:
        for op in (B2, S2, B3, B4, S4):
            wait(op, q, True)


def mixer(na, nb, shape, values, grad_mixing, factor_c, factor_a, factor_b):
    a_dev, b_dev, positions, channels = shape
    bf16, f32 = jnp.bfloat16, jnp.float32
    outer = na * a_dev
    cm = positions // (na * nb)
    rows_c = b_dev * cm
    block = a_dev * rows_c
    group = max(1, 16 // rows_c)
    rows_b = min(block, max(16, 256 // nb))
    share = rows_b // rows_c
    width = 256 if channels % 256 == 0 else channels
    chunks = channels // width
    span = group * b_dev * positions

    def eye(n):
        return jnp.eye(n, dtype=bf16)

    order = jnp.arange(span, dtype=jnp.int32).reshape(group * b_dev, na * nb, cm)
    order = order.transpose(1, 0, 2).reshape(span, 1)
    perm = (order == jnp.arange(span, dtype=jnp.int32)[None, :]).astype(bf16)
    mix_a = (
        factor_a.transpose(1, 0, 2)[:, :, None, :, None, None]
        * eye(b_dev)[None, :, None, None, :, None]
        * eye(cm)[None, None, :, None, None, :]
    ).reshape(outer * rows_c, outer * rows_c)
    wide_b = factor_b.reshape(cm, nb, b_dev, nb, b_dev).transpose(1, 2, 0, 3, 4)
    mix_b = (
        wide_b[:, None, :, :, :, None, :, None]
        * eye(share)[None, :, None, None, None, :, None, None]
        * eye(cm)[None, None, None, :, None, None, None, :]
    ).reshape(nb * rows_b, nb * rows_b)
    dims = (na, nb, a_dev, b_dev, positions, rows_c, group, rows_b, width, chunks)
    by_a = pltpu.VMEM((chunks, na, nb, block, width), bf16)
    by_b = pltpu.VMEM((chunks, nb, na, block, width), bf16)
    vmem = pl.BlockSpec(memory_space=pltpu.VMEM)
    rows = a_dev * b_dev * positions
    mixing, grad_values, gram_c, gram_a, gram_b = pl.pallas_call(
        functools.partial(mixer_kernel, dims),
        out_shape=(
            jax.ShapeDtypeStruct((rows, channels), bf16),
            jax.ShapeDtypeStruct((rows, channels), bf16),
            jax.ShapeDtypeStruct(factor_c.shape, f32),
            jax.ShapeDtypeStruct(mix_a.shape, f32),
            jax.ShapeDtypeStruct(mix_b.shape, f32),
        ),
        in_specs=[vmem] * 6,
        out_specs=(vmem,) * 5,
        scratch_shapes=[
            by_a, by_b, by_a, by_b, by_b, by_b, by_a, by_b, by_b, by_b, by_a,
            pltpu.SemaphoreType.DMA((8, chunks, max(na, nb))),
            pltpu.SemaphoreType.DMA((8, chunks, max(na, nb))),
        ],
        compiler_params=pltpu.CompilerParams(
            collective_id=0, has_side_effects=True, vmem_limit_bytes=62 * 2**20
        ),
        name="mixer",
    )(values, grad_mixing, factor_c, perm, mix_a, mix_b)
    grad_fa = jnp.einsum("kbcabc->bka", gram_a.reshape(outer, b_dev, cm, outer, b_dev, cm))
    grad_fb = jnp.einsum(
        "JgBcjgbc->cJBjb", gram_b.reshape(nb, share, b_dev, cm, nb, share, b_dev, cm)
    ).reshape(factor_b.shape)
    return mixing, grad_values, gram_c, grad_fa, grad_fb


def body(na, nb, tokens, cotangent, in_weight, out_weight, factor_c, factor_a, factor_b):
    a_dev, b_dev, positions, channels = tokens.shape
    row_count = a_dev * b_dev * positions
    grad_scale = 1.0 / math.sqrt(row_count * na * nb)
    flat_tokens = tokens.reshape(row_count, channels)
    projected = jnp.dot(flat_tokens, in_weight, preferred_element_type=jnp.float32)
    queries = projected[:, :channels].astype(jnp.bfloat16)
    values = projected[:, channels:].astype(jnp.bfloat16)
    flat_cotangent = cotangent.reshape(row_count, channels)
    query_wide = queries.astype(jnp.float32)
    sigmoid_q = jax.nn.sigmoid(query_wide)
    activation = query_wide * sigmoid_q
    slope = sigmoid_q * (1.0 + query_wide * (1.0 - sigmoid_q))
    grad_gated = product_columns(flat_cotangent, out_weight)
    grad_mixing = (grad_gated * activation).astype(jnp.bfloat16)
    mixing, grad_values, part_fc, part_fa, grad_fb = mixer(
        na, nb, tokens.shape, values, grad_mixing, factor_c, factor_a, factor_b
    )
    grad_fa = lax.psum(part_fa, "sa")
    grad_fc = lax.psum(part_fc, "sb")
    mixing_wide = mixing.astype(jnp.float32)
    gated = (activation * mixing_wide).astype(jnp.bfloat16)
    grad_queries = (grad_gated * mixing_wide * slope).astype(jnp.bfloat16)
    part_out = product_rows(gated, flat_cotangent)
    grad_projected = jnp.concatenate([grad_queries, grad_values], axis=1)
    grad_tokens = product_columns(grad_projected, in_weight).astype(jnp.bfloat16)
    part_in = product_rows(flat_tokens, grad_projected)
    sum_in, sum_out = lax.psum((part_in, part_out), ("sa", "sb"))
    return (
        grad_tokens.reshape(tokens.shape),
        sum_in * grad_scale,
        sum_out * grad_scale,
        grad_fc * grad_scale,
        grad_fa * grad_scale,
        grad_fb * grad_scale,
    )


def solution(mesh):
    return jax.shard_map(
        functools.partial(body, mesh.shape["sa"], mesh.shape["sb"]),
        mesh=mesh,
        in_specs=(
            P("sa", "sb", None, None),
            P("sa", "sb", None, None),
            P(),
            P(),
            P("sa", None, None),
            P("sb", None, None),
            P(("sa", "sb"), None, None),
        ),
        out_specs=(
            P("sa", "sb", None, None),
            P(),
            P(),
            P("sa", None, None),
            P("sb", None, None),
            P(("sa", "sb"), None, None),
        ),
        check_vma=False,
    )
```

time: 818 us -> 635 us (0.78)
  blocking collectives: 435 us -> 15.1 us
  Pallas kernels: 0 us -> 315 us
  waiting for transfers between devices: 210 us -> 144 us
  other arithmetic: 11.1 us -> 42.1 us
  matrix products: 65.3 us -> 37.8 us
  local copies, waits for them, and re-layouts: 68.9 us -> 58.6 us
    all_to_all x7 -> x0, blocking collectives: 419 us -> none  [the longest x1 76.6 us: body(): lax.all_to_all(section_two, 'sb', split_axis=2, concat_axis=1, tiled=True)]
    pallas_call x0 -> x1, Pallas kernels: none -> 315 us  [mixer(): pl.pallas_call(functools.partial(mixer_kernel, dims), out_shape=(jax.Shap...]
    all_to_all x15 -> x0, local copies, waits for them, and re-layouts: 38.4 us -> none  [the longest x3 11.1 us: body(): lax.all_to_all(section_one, 'sa', split_axis=2, concat_axis=0, tiled=True)]
    all_to_all x1 -> x0, waiting for transfers between devices: 29.9 us -> none  [body(): lax.all_to_all(grad_one, 'sa', split_axis=0, concat_axis=2, tiled=True)]
    psum x1, waiting for transfers between devices: 169 us -> 144 us  [body(): sum_in, sum_out = lax.psum((part_in, part_out), ('sa', 'sb'))]
    dot_general x9 -> x0, matrix products: 24.7 us -> none  [mix_einsum(): return jnp.einsum(formula, left, right, preferred_element_type=jnp.float32)]
    reshape x1 -> x4, local copies, waits for them, and re-layouts: 2.43 us -> 25.1 us  [the longest x1 12.5 us: mixer(): gram_a.reshape(outer, b_dev, cm, outer, b_dev, cm)]
    mul x0 -> x4, local copies, waits for them, and re-layouts: none -> 20.7 us  [the longest x1 9.52 us: mixer(): factor_a.transpose(1, 0, 2)[:, :, None, :, None, None]]
  transfers between devices with their start and end apart: 3 -> 2, of which waited for: 3 -> 1; matrix products, arithmetic and copies ran while one was open for 4% -> 11% of each run, Pallas kernels for 0% -> 0%
where the time goes in v1:
time: 635 us; the launch traced here: 627 us
  Pallas kernels  315 us (50%)
  waiting for transfers between devices  144 us (23%)
  local copies, waits for them, and re-layouts  58.6 us (9%)
  other arithmetic  42.1 us (7%)
  matrix products  37.8 us (6%)
  blocking collectives  15.1 us (2%)
  between operations  14.8 us (2%)
    pallas_call x1, Pallas kernels, mixer(): pl.pallas_call(functools.partial(mixer_kernel, dims), out_shape=(jax.Shap...  315 us
    psum x1, waiting for transfers between devices, body(): sum_in, sum_out = lax.psum((part_in, part_out), ('sa', 'sb'))  144 us
    dot_general x2, matrix products, product_columns(): lax.dot_general(left, right, CONTRACT_COLUMNS, preferred_element_type=jnp...  18.3 us
    psum x1, blocking collectives, body(): grad_fa = lax.psum(part_fa, 'sa')  15.1 us
  transfers between devices with their start and end apart: 2, of which 1 were waited for; matrix products, arithmetic and copies ran while one was open for 11% of the time, Pallas kernels for 0%

profile of v1, /device:TPU:0, one launch (start us, length us, event | category | flops | bytes accessed | tf_op | source)
XLA Modules:
  0.0 626.7 jit_solution(14840143683346091210)
XLA Ops:
  7.2 0.0 copy-start
  7.2 0.0 all-reduce.4.cloned.1.call-start
  7.3 7.5 %convolution_convert_fusion = bf16[2048,1536]{1,0:T(8,128)(2,1)S(1)} fusion(bf16[2048,768]{1,0:T(8,128)(2,1)} %bitcast.26, bf16[768,1536]{1,0:T(8,128)(2,1)} %param.9), kind=kOutput, calls=%fused_computation.7 | convolution fusion | flops 4834983936 | bytes 11796480 | tf_op jit(solution)/shard_map/dot_general | solution.py:375
  14.7 0.0 copy-start.2
  14.7 2.6 copy-done.2
  17.4 0.0 copy-start.9
  17.4 1.9 slice.10.v_ref
  19.3 0.0 copy-done.9
  19.3 0.2 broadcast_multiply_fusion.6
  19.5 0.0 copy-start.8
  19.5 3.6 broadcast_multiply_fusion.2
  23.1 9.5 %mul.135.ma_ref = bf16[256,256]{1,0:T(8,128)(2,1)} reshape(bf16[16,4,4,16,4,4]{5,4,3,2,1,0:T(4,128)(2,1)} %broadcast_multiply_fusion.2) | data formatting | bytes 262144 | tf_op jit(solution)/shard_map/mul | solution.py:327
  32.6 0.0 copy-done.8
  32.6 0.2 reshape.142
  32.8 1.2 broadcast_multiply_fusion.4
  34.1 6.2 broadcast_multiply_fusion.1
  40.3 9.5 %mul.142.mb_ref = bf16[256,256]{1,0:T(8,128)(2,1)} reshape(bf16[8,2,4,4,8,2,4,4]{7,6,5,4,3,2,1,0:T(4,128)(2,1)} %broadcast_multiply_fusion.1) | data formatting | bytes 262144 | tf_op jit(solution)/shard_map/mul | solution.py:333
  49.8 0.1 reshape.141
  50.0 1.0 fusion.14.perm_ref
  50.9 0.0 copy-done
  50.9 9.9 %multiply_convert_fusion = (bf16[2048,768]{1,0:T(8,128)(2,1)}, f32[2048,768]{1,0:T(8,128)}) fusion(bf16[2048,1536]{1,0:T(8,128)(2,1)} %copy-done.2, bf16[2048,768]{1,0:T(8,128)(2,1)} %bitcast.28, bf16[768,768]{1,0:T(8,128)(2,1)S(1)} %copy-done), kind=kOutput, calls=%fused_computation.17 | convolution fusion | flops 2426929152 | bytes 16908288 | tf_op jit(solution)/shard_map/dot_general | solution.py:21
  60.8 314.6 %mixer.1 = (bf16[2048,768]{1,0:T(8,128)(2,1)}, bf16[2048,768]{1,0:T(8,128)(2,1)}, f32[4,128,128]{2,1,0:T(8,128)}, f32[256,256]{1,0:T(8,128)}, f32[256,256]{1,0:T(8,128)}) custom-call(bf16[2048,768]{1,0:T(8,128)(2,1)} %slice.10.v_ref, bf16[2048,768]{1,0:T(8,128)(2,1)} %get-tuple-element.42.g_ref, bf16[4,128,128]{2,1,0:T(8,128)(2,1)} %fc_ref.1, ...), custom_call_target="tpu_custom_call" | custom-call | tf_op jit(solution)/shard_map/mixer/pallas_call | solution.py:342
  375.5 0.0 all-reduce.4.cloned.1.call-update
  375.5 0.0 all-reduce.6.cloned.1.call-start
  375.6 0.0 copy-start.10
  375.6 0.0 copy-start.12
  375.6 0.0 slice-start
  375.6 6.3 %fusion.1 = bf16[2048,768]{1,0:T(8,128)(2,1)S(1)} fusion(f32[2048,768]{1,0:T(8,128)} %get-tuple-element.43, bf16[2048,768]{1,0:T(8,128)(2,1)} %get-tuple-element.11, bf16[2048,1536]{1,0:T(8,128)(2,1)} %copy-done.2), kind=kLoop, calls=%fused_computation.9 | loop fusion | flops 18874368 | bytes 15728640 | tf_op jit(solution)/shard_map/convert_element_type | solution.py:392
  382.0 0.0 copy-start.3
  382.0 0.0 copy-done.10
  382.0 0.1 copy-done.12
  382.1 7.3 %fusion.10 = f32[768,1536]{0,1:T(8,128)} fusion(bf16[2048,768]{1,0:T(8,128)(2,1)S(1)} %bitcast.27, bf16[2048,768]{1,0:T(8,128)(2,1)S(1)} %copy-done.12, bf16[2048,768]{1,0:T(8,128)(2,1)S(1)} %fusion.1), kind=kOutput, calls=%fused_computation.20 | convolution fusion | flops 4844421120 | bytes 14155776 | tf_op jit(solution)/shard_map/dot_general | solution.py:17
  389.4 0.0 copy-done.3
  389.4 0.0 slice-done
  389.4 0.0 slice-done.1
  389.4 0.0 copy-done.4
  389.4 0.0 copy-done.11
  389.4 4.7 fusion.12
  394.2 0.0 all-reduce.6.cloned.1.call-update
  394.2 0.9 copy-done.7
  395.1 12.5 %reshape.144 = f32[16,4,4,16,4,4]{5,4,3,2,1,0:T(4,128)} reshape(f32[256,256]{1,0:T(8,128)S(1)} %copy-done.7) | data formatting | bytes 524288 | tf_op jit(solution)/shard_map/reshape | solution.py:363
  407.6 0.0 copy-start.6
  407.6 6.6 %select_reduce_fusion.1 = f32[16,4,16,4,4]{4,3,2,1,0:T(4,128)S(1)} fusion(f32[16,4,4,16,4,4]{5,4,3,2,1,0:T(4,128)} %reshape.144, pred[4,4]{1,0:T(4,128)(4,1)S(1)} %iota_compare_fusion.1), kind=kLoop, calls=%fused_computation.4 | loop fusion | flops 114688 | bytes 327696 | tf_op jit(solution)/shard_map/kbcabc->bka/reduce_sum | solution.py:363
  414.2 0.6 select_reduce_fusion.3
  414.9 0.2 copy.43
  415.0 0.0 copy-done.6
  415.0 12.3 %reshape.145 = f32[8,2,4,4,8,2,4,4]{7,6,5,4,3,2,1,0:T(4,128)} reshape(f32[256,256]{1,0:T(8,128)S(1)} %copy-done.6) | data formatting | bytes 524288 | tf_op jit(solution)/shard_map/reshape | solution.py:365
  427.3 6.8 %select_reduce_fusion = f32[8,4,4,8,4,4]{5,4,3,2,1,0:T(4,128)S(1)} fusion(f32[8,2,4,4,8,2,4,4]{7,6,5,4,3,2,1,0:T(4,128)} %reshape.145, pred[2,2]{1,0:T(4,128)(4,1)S(1)} %iota_compare_fusion.3), kind=kLoop, calls=%fused_computation.3 | loop fusion | flops 114688 | bytes 327684 | tf_op jit(solution)/shard_map/JgBcjgbc->cJBjb/reduce_sum | solution.py:364
  434.1 0.0 copy-start.13
  434.1 0.7 select_reduce_fusion.2
  434.9 0.9 copy.44
  435.8 0.8 copy.39
  436.6 0.8 mul.159
  437.4 15.1 %psum.31 = f32[4,16,16]{2,1,0:T(8,128)S(1)} all-reduce(f32[4,16,16]{2,1,0:T(8,128)S(1)} %bitcast.24), channel_id=1, replica_groups=mesh['sa'=4,'sb'=8] {'sa'}, use_global_device_ids=true, to_apply=%region_5.0 | all-reduce | flops 1024 | bytes 8192 | tf_op jit(solution)/shard_map/psum | solution.py:388
  452.5 0.6 broadcast_multiply_fusion.7
  453.1 0.0 copy-done.13
  453.1 8.4 %fusion.11 = bf16[2048,768]{1,0:T(8,128)(2,1)} fusion(bf16[768,1536]{1,0:T(8,128)(2,1)S(1)} %copy-done.13, bf16[2048,768]{1,0:T(8,128)(2,1)} %get-tuple-element.12, bf16[2048,768]{1,0:T(8,128)(2,1)} %copy-done.3), kind=kOutput, calls=%fused_computation.21 | convolution fusion | flops 4845993984 | bytes 11796480 | tf_op jit(solution)/shard_map/dot_general | solution.py:21
  461.5 1.7 broadcast_multiply_fusion.5
  463.2 143.6 %all-reduce.6.cloned.1.call-done = (f32[768,1536]{0,1:T(8,128)}, f32[768,768]{1,0:T(8,128)}) async-done(((f32[768,1536]{0,1:T(8,128)}, f32[768,768]{1,0:T(8,128)}), (f32[768,1536]{0,1:T(8,128)}, f32[768,768]{1,0:T(8,128)})) %all-reduce.6.cloned.1.call-update) | async-done | bytes 7077904 | tf_op jit(solution)/shard_map/psum | solution.py:397
  606.8 4.8 broadcast_multiply_fusion
  611.6 6.2 copy.40
  617.8 0.0 copy-done.5
  617.8 1.6 broadcast_multiply_fusion.3
  619.4 0.0 copy-done.1
  (15 shorter events, 0.1 us)
Async XLA Ops:
  7.2 43.7 %copy-start = (bf16[768,768]{1,0:T(8,128)(2,1)S(1)}, bf16[768,768]{1,0:T(8,128)(2,1)}, u32[]{:S(2)}) copy-start(bf16[768,768]{1,0:T(8,128)(2,1)} %param.10) | copy-start | bytes 3538948
  7.2 454.3 %all-reduce.4.cloned.1.call-start = ((), (), s32[]{:S(2)}) async-start(), calls=%async_computation | async-start | bytes 524288 | tf_op jit(solution)/shard_map/psum | solution.py:389
  14.7 2.7 copy-start.2
  17.4 1.9 copy-start.9
  19.5 13.2 %copy-start.8 = (bf16[4,32,32]{2,1,0:T(8,128)(2,1)S(1)}, bf16[4,32,32]{2,1,0:T(8,128)(2,1)}, u32[]{:S(2)}) copy-start(bf16[4,32,32]{2,1,0:T(8,128)(2,1)} %param.13) | copy-start | bytes 24580
  375.5 231.3 %all-reduce.6.cloned.1.call-start = ((), (), s32[]{:S(2)}) async-start(), calls=%async_computation.1 | async-start | bytes 14155776 | tf_op jit(solution)/shard_map/psum | solution.py:397
  375.6 6.4 %copy-start.10 = (bf16[4,4,128,768]{3,2,1,0:T(8,128)(2,1)S(1)}, bf16[4,4,128,768]{3,2,1,0:T(8,128)(2,1)}, u32[]{:S(2)}) copy-start(bf16[4,4,128,768]{3,2,1,0:T(8,128)(2,1)} %param.7) | copy-start | bytes 9437188
  375.6 6.5 %copy-start.12 = (bf16[2048,768]{1,0:T(8,128)(2,1)S(1)}, bf16[2048,768]{1,0:T(8,128)(2,1)}, u32[]{:S(2)}) copy-start(bf16[2048,768]{1,0:T(8,128)(2,1)} %get-tuple-element.12) | copy-start | bytes 9437188
  375.6 13.8 %slice-start = ((s8[6291456]{0:T(1024)(128)(4,1)}), s8[4194304]{0:T(1024)(128)(4,1)S(1)}, s32[]{:S(2)}) async-start(s8[6291456]{0:T(1024)(128)(4,1)} %bitcast.22), calls=%async_computation.2 | async-start | bytes 8388608
  382.0 7.4 %copy-start.3 = (bf16[2048,768]{1,0:T(8,128)(2,1)}, bf16[2048,768]{1,0:T(8,128)(2,1)S(1)}, u32[]{:S(2)}) copy-start(bf16[2048,768]{1,0:T(8,128)(2,1)S(1)} %fusion.1) | copy-start | bytes 9437188
  382.1 7.3 %slice-start.1 = ((s8[6291456]{0:T(1024)(128)(4,1)}), s8[2097152]{0:T(1024)(128)(4,1)S(1)}, s32[]{:S(2)}) async-start(s8[6291456]{0:T(1024)(128)(4,1)} %bitcast.22), calls=%async_computation.3 | async-start | bytes 4194304
  382.1 7.3 %copy-start.4 = (bf16[2048,768]{1,0:T(8,128)(2,1)S(1)}, bf16[2048,768]{1,0:T(8,128)(2,1)}, u32[]{:S(2)}) copy-start(bf16[2048,768]{1,0:T(8,128)(2,1)} %get-tuple-element.11) | copy-start | bytes 9437188
  382.1 7.3 %copy-start.11 = (bf16[4,4,128,768]{3,2,1,0:T(8,128)(2,1)S(1)}, bf16[4,4,128,768]{3,2,1,0:T(8,128)(2,1)}, u32[]{:S(2)}) copy-start(bf16[4,4,128,768]{3,2,1,0:T(8,128)(2,1)} %param.8) | copy-start | bytes 9437188
  394.2 1.0 copy-start.7
  407.6 7.4 %copy-start.6 = (f32[256,256]{1,0:T(8,128)S(1)}, f32[256,256]{1,0:T(8,128)}, u32[]{:S(2)}) copy-start(f32[256,256]{1,0:T(8,128)} %get-tuple-element.15) | copy-start | bytes 786436
  434.1 19.0 %copy-start.13 = (bf16[768,1536]{1,0:T(8,128)(2,1)S(1)}, bf16[768,1536]{1,0:T(8,128)(2,1)}, u32[]{:S(2)}) copy-start(bf16[768,1536]{1,0:T(8,128)(2,1)} %param.9) | copy-start | bytes 7077892
  611.6 6.2 copy-start.5
  611.6 7.8 %copy-start.1 = (bf16[768,768]{1,0:T(8,128)(2,1)S(1)}, bf16[768,768]{1,0:T(8,128)(2,1)}, u32[]{:S(2)}) copy-start(bf16[768,768]{1,0:T(8,128)(2,1)} %param.10) | copy-start | bytes 3538948
Sparse Core Ops, SparseCore 0:
  375.6 60.3 all-reduce.3
  443.6 163.2 all-reduce.5

commit v2 on v1

--- a/solution.py
+++ b/solution.py
@@ -317,23 +317,22 @@
     chunks = channels // width
     span = group * b_dev * positions
 
-    def eye(n):
-        return jnp.eye(n, dtype=bf16)
-
     order = jnp.arange(span, dtype=jnp.int32).reshape(group * b_dev, na * nb, cm)
     order = order.transpose(1, 0, 2).reshape(span, 1)
     perm = (order == jnp.arange(span, dtype=jnp.int32)[None, :]).astype(bf16)
-    mix_a = (
-        factor_a.transpose(1, 0, 2)[:, :, None, :, None, None]
-        * eye(b_dev)[None, :, None, None, :, None]
-        * eye(cm)[None, None, :, None, None, :]
-    ).reshape(outer * rows_c, outer * rows_c)
-    wide_b = factor_b.reshape(cm, nb, b_dev, nb, b_dev).transpose(1, 2, 0, 3, 4)
-    mix_b = (
-        wide_b[:, None, :, :, :, None, :, None]
-        * eye(share)[None, :, None, None, None, :, None, None]
-        * eye(cm)[None, None, None, :, None, None, None, :]
-    ).reshape(nb * rows_b, nb * rows_b)
+    at_a = jnp.arange(outer * rows_c, dtype=jnp.int32)
+    same_a = at_a[:, None] % rows_c == at_a[None, :] % rows_c
+    wide_a = (jnp.arange(outer, dtype=jnp.int32)[:, None] == at_a[None, :] // rows_c).astype(bf16)
+    at_b = jnp.arange(nb * rows_b, dtype=jnp.int32)
+    inner_b = at_b // rows_b * b_dev + at_b // cm % b_dev
+    kind_b = at_b % rows_b // rows_c * cm + at_b % cm
+    same_b = kind_b[:, None] == kind_b[None, :]
+    wide_b = (jnp.arange(nb * b_dev, dtype=jnp.int32)[:, None] == inner_b[None, :]).astype(bf16)
+    rows_fa = jnp.repeat(factor_a.transpose(1, 0, 2).reshape(outer * b_dev, outer), cm, axis=0)
+    mix_a = jnp.where(same_a, product(rows_fa, wide_a), 0.0).astype(bf16)
+    rows_fb = factor_b.reshape(cm, nb, 1, b_dev, nb * b_dev).transpose(1, 2, 3, 0, 4)
+    rows_fb = jnp.broadcast_to(rows_fb, (nb, share, b_dev, cm, nb * b_dev)).reshape(nb * rows_b, nb * b_dev)
+    mix_b = jnp.where(same_b, product(rows_fb, wide_b), 0.0).astype(bf16)
     dims = (na, nb, a_dev, b_dev, positions, rows_c, group, rows_b, width, chunks)
     by_a = pltpu.VMEM((chunks, na, nb, block, width), bf16)
     by_b = pltpu.VMEM((chunks, nb, na, block, width), bf16)
@@ -360,12 +359,166 @@
         ),
         name="mixer",
     )(values, grad_mixing, factor_c, perm, mix_a, mix_b)
-    grad_fa = jnp.einsum("kbcabc->bka", gram_a.reshape(outer, b_dev, cm, outer, b_dev, cm))
-    grad_fb = jnp.einsum(
-        "JgBcjgbc->cJBjb", gram_b.reshape(nb, share, b_dev, cm, nb, share, b_dev, cm)
-    ).reshape(factor_b.shape)
+    def narrow(gram, same, wide):
+        return lax.dot_general(
+            jnp.where(same, gram, 0.0), wide.astype(f32), CONTRACT_COLUMNS,
+            precision=lax.Precision.HIGHEST, preferred_element_type=f32,
+        )
+
+    grad_fa = narrow(gram_a, same_a, wide_a).reshape(outer, b_dev, cm, outer).sum(axis=2).transpose(1, 0, 2)
+    grad_fb = narrow(gram_b, same_b, wide_b).reshape(nb, share, b_dev, cm, nb * b_dev).sum(axis=1)
+    grad_fb = grad_fb.transpose(2, 0, 1, 3).reshape(factor_b.shape)
     return mixing, grad_values, gram_c, grad_fa, grad_fb
 
+
+def total_kernel(na, nz, chunks, x_ref, out_ref, r0, s0, r1, s1, r2, send_sem, recv_sem):
+    me_a = lax.axis_index("sa")
+    me_b = lax.axis_index("sb")
+    core, me_z = lax.rem(me_b, 2), lax.div(me_b, 2)
+    other = 1 - core
+    width = x_ref.shape[-1] // chunks
+    bf16, f32 = jnp.bfloat16, jnp.float32
+    mesh_ids = pl.DeviceIdType.MESH
+
+    def to_a(t):
+        return lax.rem(me_a + t, na)
+
+    def to_z(t):
+        return lax.rem(me_z + t, nz)
+
+    def on_z(z):
+        return {"sb": z * 2 + core}
+
+    barrier = pltpu.get_barrier_semaphore()
+
+    def greet_a(t, carry):
+        pl.semaphore_signal(barrier, inc=1, device_id={"sa": to_a(t)}, device_id_type=mesh_ids)
+        return carry
+
+    def greet_z(t, carry):
+        pl.semaphore_signal(barrier, inc=1, device_id=on_z(to_z(t)), device_id_type=mesh_ids)
+        return carry
+
+    lax.fori_loop(1, na, greet_a, 0)
+    lax.fori_loop(1, nz, greet_z, 0)
+    pl.semaphore_signal(barrier, inc=1, device_id={"sb": me_z * 2 + other}, device_id_type=mesh_ids)
+    pl.semaphore_wait(barrier, na + nz - 1)
+
+    def columns(q):
+        return slice(q * width, (q + 1) * width)
+
+    def copy(stage, q, peer, slot):
+        cols = columns(q)
+        if stage == 0:
+            src, dst, target = x_ref.at[other, :, :, :, cols], r0.at[q], {"sb": me_z * 2 + other}
+        elif stage == 1:
+            src, dst, target = s0.at[q, peer], r1.at[q, slot], {"sa": peer}
+        elif stage == 2:
+            src, dst, target = s1.at[q, peer], r2.at[q, slot], on_z(peer)
+        elif stage == 3:
+            src, dst = out_ref.at[core, me_a, me_z, :, cols], out_ref.at[core, me_a, slot, :, cols]
+            target = on_z(peer)
+        elif stage == 4:
+            src, dst = out_ref.at[core, me_a, :, :, cols], out_ref.at[core, slot, :, :, cols]
+            target = {"sa": peer}
+        else:
+            src, dst = out_ref.at[core, :, :, :, cols], out_ref.at[slot, :, :, :, cols]
+            target = {"sb": me_z * 2 + other}
+        return pltpu.make_async_remote_copy(
+            src_ref=src, dst_ref=dst, send_sem=send_sem.at[stage, q, peer], recv_sem=recv_sem.at[stage, q, slot],
+            device_id=target, device_id_type=mesh_ids,
+        )
+
+    def each(stage, act):
+        if stage in (0, 5):
+            act(other, core)
+            return
+        size, peer_of, me = (na, to_a, me_a) if stage in (1, 4) else (nz, to_z, me_z)
+
+        def one(t, carry):
+            act(peer_of(t), me)
+            return carry
+
+        lax.fori_loop(1, size, one, 0)
+
+    def start(stage, q):
+        each(stage, lambda peer, me: copy(stage, q, peer, me).start())
+
+    def arrive(stage, q):
+        each(stage, lambda peer, me: copy(stage, q, peer, peer).wait_recv())
+
+    every = range(chunks)
+    for q in every:
+        start(0, q)
+    for q in every:
+        arrive(0, q)
+
+        def pair(i, carry):
+            s0[q, i] = (x_ref[core, i, :, :, columns(q)].astype(f32) + r0[q, i].astype(f32)).astype(bf16)
+            return carry
+
+        lax.fori_loop(0, na, pair, 0)
+        start(1, q)
+    for q in every:
+        arrive(1, q)
+
+        def across(z, carry):
+            total = s0[q, me_a, z].astype(f32)
+            for t in range(1, na):
+                total += r1[q, to_a(t), z].astype(f32)
+            s1[q, z] = total.astype(bf16)
+            return carry
+
+        lax.fori_loop(0, nz, across, 0)
+        start(2, q)
+    for q in every:
+        arrive(2, q)
+        total = s1[q, me_z].astype(f32)
+        for t in range(1, nz):
+            total += r2[q, to_z(t)].astype(f32)
+        out_ref[core, me_a, me_z, :, columns(q)] = total.astype(bf16)
+        start(3, q)
+    for q in every:
+        arrive(3, q)
+        start(4, q)
+    for q in every:
+        arrive(4, q)
+        start(5, q)
+    for q in every:
+        arrive(5, q)
+    for q in every:
+        for stage in range(6):
+            each(stage, lambda peer, me: copy(stage, q, peer, me).wait_send())
+
+
+def total(na, nb, parts):
+    nz = nb // 2
+    rows, channels = sum(part.shape[0] for part in parts), parts[0].shape[1]
+    share = -(-rows // (na * nb * 16)) * 16
+    filler = jnp.zeros((share * na * nb - rows, channels), jnp.bfloat16)
+    stacked = jnp.concatenate([*parts, filler], axis=0).reshape(2, na, nz, share, channels)
+    chunks = channels // 256 if channels % 256 == 0 else 1
+    width = channels // chunks
+    vmem = pl.BlockSpec(memory_space=pltpu.VMEM)
+    by_a = pltpu.VMEM((chunks, na, nz, share, width), jnp.bfloat16)
+    by_z = pltpu.VMEM((chunks, nz, share, width), jnp.bfloat16)
+    sems = pltpu.SemaphoreType.DMA((6, chunks, max(na, nz, 2)))
+    summed = pl.pallas_call(
+        functools.partial(total_kernel, na, nz, chunks),
+        out_shape=jax.ShapeDtypeStruct(stacked.shape, jnp.bfloat16),
+        in_specs=[vmem],
+        out_specs=vmem,
+        scratch_shapes=[by_a, by_a, by_a, by_z, by_z, sems, sems],
+        compiler_params=pltpu.CompilerParams(
+            collective_id=1, has_side_effects=True, vmem_limit_bytes=48 * 2**20
+        ),
+        name="total",
+    )(stacked).reshape(share * na * nb, channels)
+    ends, begin = [], 0
+    for part in parts:
+        ends.append(summed[begin : begin + part.shape[0]].astype(jnp.float32))
+        begin += part.shape[0]
+    return ends
 
 def body(na, nb, tokens, cotangent, in_weight, out_weight, factor_c, factor_a, factor_b):
     a_dev, b_dev, positions, channels = tokens.shape
@@ -390,11 +543,13 @@
     mixing_wide = mixing.astype(jnp.float32)
     gated = (activation * mixing_wide).astype(jnp.bfloat16)
     grad_queries = (grad_gated * mixing_wide * slope).astype(jnp.bfloat16)
-    part_out = product_rows(gated, flat_cotangent)
+    part_out = product_rows(gated, flat_cotangent).astype(jnp.bfloat16)
+    part_queries = product_rows(flat_tokens, grad_queries).astype(jnp.bfloat16)
+    part_values = product_rows(flat_tokens, grad_values).astype(jnp.bfloat16)
     grad_projected = jnp.concatenate([grad_queries, grad_values], axis=1)
     grad_tokens = product_columns(grad_projected, in_weight).astype(jnp.bfloat16)
-    part_in = product_rows(flat_tokens, grad_projected)
-    sum_in, sum_out = lax.psum((part_in, part_out), ("sa", "sb"))
+    sum_out, sum_queries, sum_values = total(na, nb, (part_out, part_queries, part_values))
+    sum_in = jnp.concatenate([sum_queries, sum_values], axis=1)
     return (
         grad_tokens.reshape(tokens.shape),
         sum_in * grad_scale,

time: 635 us -> 486 us (0.77); the launches traced: 627 us -> 485 us
  waiting for transfers between devices: 144 us -> 0.02 us
  Pallas kernels: 315 us -> 384 us
  local copies, waits for them, and re-layouts: 58.6 us -> 6 us
  other arithmetic: 42.1 us -> 22.1 us
    psum x1 -> x0, waiting for transfers between devices: 144 us -> none  [body(): sum_in, sum_out = lax.psum((part_in, part_out), ('sa', 'sb'))]
    pallas_call x0 -> x1, Pallas kernels: none -> 69.1 us  [total(): pl.pallas_call(functools.partial(total_kernel, na, nz, chunks), out_shape...]
    reshape x3 -> x0, local copies, waits for them, and re-layouts: 25 us -> none  [the longest x1 12.5 us: mixer(): gram_a.reshape(outer, b_dev, cm, outer, b_dev, cm)]
    mul x4 -> x0, local copies, waits for them, and re-layouts: 20.7 us -> none  [the longest x1 9.52 us: mixer(): factor_a.transpose(1, 0, 2)[:, :, None, :, None, None]]
    reduce_sum x4 -> x2, other arithmetic: 14.8 us -> 3.19 us  [the longest x1 1.61 us: mixer(): narrow(gram_a, same_a, wide_a).reshape(outer, b_dev, cm, outer).sum(axis=2)]
    mul x4 -> x0, other arithmetic: 11.3 us -> none  [the longest x2 7.48 us: mixer(): wide_b[:, None, :, :, :, None, :, None]]
    unnamed x35 -> x22, local copies, waits for them, and re-layouts: 11 us -> 3.64 us
  transfers between devices with their start and end apart: 2 -> 1, of which waited for: 1 -> 0; matrix products, arithmetic and copies ran while one was open for 11% -> 9% of each run, Pallas kernels for 0% -> 14%
where the time goes in v2:
time: 486 us; the launch traced here: 485 us
  Pallas kernels  384 us (79%)
  matrix products  40.9 us (8%)
  other arithmetic  22.1 us (5%)
  blocking collectives  18.1 us (4%)
  between operations  14.3 us (3%)
  local copies, waits for them, and re-layouts  6 us (1%)
    pallas_call x1, Pallas kernels, mixer(): pl.pallas_call(functools.partial(mixer_kernel, dims), out_shape=(jax.Shap...  315 us
    pallas_call x1, Pallas kernels, total(): pl.pallas_call(functools.partial(total_kernel, na, nz, chunks), out_shape...  69.1 us
    psum x1, blocking collectives, body(): grad_fa = lax.psum(part_fa, 'sa')  18.1 us
    dot_general x2, matrix products, product_columns(): lax.dot_general(left, right, CONTRACT_COLUMNS, preferred_element_type=jnp...  16.4 us
    dot_general x3, matrix products, product_rows(): lax.dot_general(left, right, CONTRACT_ROWS, preferred_element_type=jnp.fl...  12.5 us
  transfers between devices with their start and end apart: 1, of which 0 were waited for; matrix products, arithmetic and copies ran while one was open for 9% of the time, Pallas kernels for 14%

profile of v2, /device:TPU:0, one launch (start us, length us, event | category | flops | bytes accessed | tf_op | source)
XLA Modules:
  0.0 485.3 jit_solution(11720756422300863764)
XLA Ops:
  7.2 0.0 copy-start
  7.2 0.0 all-reduce.2.cloned.1.call-start
  7.3 7.5 %convolution_convert_fusion = bf16[2048,1536]{1,0:T(8,128)(2,1)S(1)} fusion(bf16[2048,768]{1,0:T(8,128)(2,1)} %bitcast.62, bf16[768,1536]{1,0:T(8,128)(2,1)} %param.9), kind=kOutput, calls=%fused_computation.5 | convolution fusion | flops 4834983936 | bytes 11796480 | tf_op jit(solution)/shard_map/dot_general | solution.py:528
  14.7 0.0 copy-start.1
  14.7 0.0 copy-start.5
  14.8 0.0 copy-start.6
  14.8 2.0 slice.22.v_ref
  16.8 1.6 copy-done.1
  18.3 0.0 copy-done.5
  18.4 0.0 copy-done.6
  18.4 0.1 reshape.265
  18.5 1.0 fusion.26.perm_ref
  19.5 0.0 copy-done
  19.5 9.9 %multiply_convert_fusion = (bf16[2048,768]{1,0:T(8,128)(2,1)}, f32[2048,768]{1,0:T(8,128)}) fusion(bf16[2048,1536]{1,0:T(8,128)(2,1)} %copy-done.1, bf16[2048,768]{1,0:T(8,128)(2,1)} %bitcast.60, bf16[768,768]{1,0:T(8,128)(2,1)S(1)} %copy-done), kind=kOutput, calls=%fused_computation.18 | convolution fusion | flops 2426929152 | bytes 16908288 | tf_op jit(solution)/shard_map/dot_general | solution.py:21
  29.4 0.8 fusion.25.mb_ref
  30.3 0.8 fusion.24.ma_ref
  31.1 314.8 %mixer.1 = (bf16[2048,768]{1,0:T(8,128)(2,1)}, bf16[2048,768]{1,0:T(8,128)(2,1)}, f32[4,128,128]{2,1,0:T(8,128)}, f32[256,256]{1,0:T(8,128)}, f32[256,256]{1,0:T(8,128)}) custom-call(bf16[2048,768]{1,0:T(8,128)(2,1)} %slice.22.v_ref, bf16[2048,768]{1,0:T(8,128)(2,1)} %get-tuple-element.24.g_ref, bf16[4,128,128]{2,1,0:T(8,128)(2,1)} %fc_ref.1, ...), custom_call_target="tpu_custom_call" | custom-call | tf_op jit(solution)/shard_map/mixer/pallas_call | solution.py:341
  345.9 0.0 all-reduce.2.cloned.1.call-update
  345.9 0.0 copy-start.2
  346.0 7.2 %fusion.17 = bf16[768,768]{1,0:T(8,128)(2,1)S(1)} fusion(bf16[2048,768]{1,0:T(8,128)(2,1)} %bitcast.61, bf16[2048,768]{1,0:T(8,128)(2,1)} %get-tuple-element.11, bf16[2048,1536]{1,0:T(8,128)(2,1)} %copy-done.1), kind=kOutput, calls=%fused_computation.24 | convolution fusion | flops 2429091840 | bytes 10616832 | tf_op jit(solution)/shard_map/dot_general | solution.py:17
  353.1 0.0 copy-done.2
  353.1 0.0 copy-start.7
  353.2 5.2 %fusion.1 = bf16[2048,768]{1,0:T(8,128)(2,1)S(1)} fusion(f32[2048,768]{1,0:T(8,128)} %get-tuple-element.25, bf16[2048,768]{1,0:T(8,128)(2,1)S(1)} %copy-done.2, bf16[2048,1536]{1,0:T(8,128)(2,1)} %copy-done.1), kind=kLoop, calls=%fused_computation.7 | loop fusion | flops 18874368 | bytes 15728640 | tf_op jit(solution)/shard_map/convert_element_type | solution.py:545
  358.4 0.0 copy-done.7
  358.4 0.0 copy-start.8
  358.4 2.7 fusion.20
  361.1 0.0 copy-done.8
  361.1 2.7 fusion.21
  363.8 5.7 %maximum_maximum_fusion = bf16[2560,768]{1,0:T(8,128)(2,1)} fusion(bf16[768,768]{1,0:T(8,128)(2,1)S(1)} %fusion.21, bf16[768,768]{1,0:T(8,128)(2,1)S(1)} %fusion.20, bf16[768,768]{1,0:T(8,128)(2,1)S(1)} %fusion.17, bf16[2560]{0:T(1024)(128)(2,1)S(1)} %pad.5.clone), kind=kLoop, calls=%fused_computation.20 | loop fusion | flops 15728640 | bytes 7476224 | tf_op jit(solution)/shard_map/concatenate | solution.py:499
  369.5 69.1 %total.1 = bf16[2,4,4,80,768]{4,3,2,1,0:T(8,128)(2,1)S(1)} custom-call(bf16[2,4,4,80,768]{4,3,2,1,0:T(8,128)(2,1)} %bitcast.50), custom_call_target="tpu_custom_call" | custom-call | tf_op jit(solution)/shard_map/total/pallas_call | solution.py:506
  438.7 0.0 copy-start.9
  438.7 0.2 fusion.51
  438.8 1.6 convert_multiply_fusion.5
  440.4 0.8 copy-done.9
  441.2 0.0 copy-start.3
  441.2 6.4 %fusion.12 = bf16[2048,768]{1,0:T(8,128)(2,1)} fusion(bf16[768,1536]{1,0:T(8,128)(2,1)S(1)} %copy-done.9, bf16[2048,768]{1,0:T(8,128)(2,1)S(1)} %copy-done.8, bf16[2048,768]{1,0:T(8,128)(2,1)S(1)} %fusion.1), kind=kOutput, calls=%fused_computation.21 | convolution fusion | flops 4845993984 | bytes 11796480 | tf_op jit(solution)/shard_map/dot_general | solution.py:21
  447.6 0.0 copy-done.3
  447.6 1.0 fusion.28
  448.6 1.6 reduce_sum.19
  450.2 0.9 broadcast_multiply_fusion.1
  451.0 0.6 copy.38
  451.7 1.9 fusion.27
  453.6 1.6 reduce_sum.18
  455.2 18.1 %psum.15 = f32[4,16,16]{2,0,1:T(4,128)} all-reduce(f32[4,16,16]{2,0,1:T(4,128)} %bitcast.54), channel_id=1, replica_groups=mesh['sa'=4,'sb'=8] {'sa'}, use_global_device_ids=true, to_apply=%region_2.3 | all-reduce | flops 1024 | bytes 8192 | tf_op jit(solution)/shard_map/psum | solution.py:541
  473.4 0.0 copy-start.4
  473.4 2.8 convert_multiply_fusion.4
  476.2 0.0 copy-done.4
  476.2 0.6 copy.37
  476.8 0.0 all-reduce.2.cloned.1.call-done
  476.8 1.7 broadcast_multiply_fusion
  (10 shorter events, 0.1 us)
Async XLA Ops:
  7.2 12.3 %copy-start = (bf16[768,768]{1,0:T(8,128)(2,1)S(1)}, bf16[768,768]{1,0:T(8,128)(2,1)}, u32[]{:S(2)}) copy-start(bf16[768,768]{1,0:T(8,128)(2,1)} %param.10) | copy-start | bytes 3538948
  7.2 469.6 %all-reduce.2.cloned.1.call-start = ((), (), s32[]{:S(2)}) async-start(), calls=%async_computation | async-start | bytes 524288 | tf_op jit(solution)/shard_map/psum | solution.py:542
  14.7 3.6 copy-start.1
  14.7 3.6 copy-start.5
  14.8 3.6 copy-start.6
  345.9 7.2 %copy-start.2 = (bf16[2048,768]{1,0:T(8,128)(2,1)S(1)}, bf16[2048,768]{1,0:T(8,128)(2,1)}, u32[]{:S(2)}) copy-start(bf16[2048,768]{1,0:T(8,128)(2,1)} %get-tuple-element.11) | copy-start | bytes 9437188
  353.1 5.3 %copy-start.7 = (bf16[4,4,128,768]{3,2,1,0:T(8,128)(2,1)S(1)}, bf16[4,4,128,768]{3,2,1,0:T(8,128)(2,1)}, u32[]{:S(2)}) copy-start(bf16[4,4,128,768]{3,2,1,0:T(8,128)(2,1)} %param.7) | copy-start | bytes 9437188
  358.4 2.7 copy-start.8
  438.7 2.5 copy-start.9
  441.2 6.4 %copy-start.3 = (f32[256,256]{1,0:T(8,128)S(1)}, f32[256,256]{1,0:T(8,128)}, u32[]{:S(2)}) copy-start(f32[256,256]{1,0:T(8,128)} %get-tuple-element.15) | copy-start | bytes 786436
  473.4 2.8 copy-start.4
Sparse Core Ops, SparseCore 0:
  346.1 60.8 all-reduce.1

commit v3 on v2

--- a/solution.py
+++ b/solution.py
@@ -538,7 +538,11 @@
     mixing, grad_values, part_fc, part_fa, grad_fb = mixer(
         na, nb, tokens.shape, values, grad_mixing, factor_c, factor_a, factor_b
     )
-    grad_fa = lax.psum(part_fa, "sa")
+    me_b = lax.axis_index("sb")
+    fa_rows = -(-part_fa.size // channels)
+    flat_fa = jnp.pad(part_fa.reshape(-1), (0, fa_rows * channels - part_fa.size)).reshape(1, fa_rows, channels)
+    mine = (jnp.arange(nb, dtype=jnp.int32) == me_b)[:, None, None]
+    placed_fa = jnp.where(mine, flat_fa, 0.0).astype(jnp.bfloat16).reshape(nb * fa_rows, channels)
     grad_fc = lax.psum(part_fc, "sb")
     mixing_wide = mixing.astype(jnp.float32)
     gated = (activation * mixing_wide).astype(jnp.bfloat16)
@@ -548,7 +552,9 @@
     part_values = product_rows(flat_tokens, grad_values).astype(jnp.bfloat16)
     grad_projected = jnp.concatenate([grad_queries, grad_values], axis=1)
     grad_tokens = product_columns(grad_projected, in_weight).astype(jnp.bfloat16)
-    sum_out, sum_queries, sum_values = total(na, nb, (part_out, part_queries, part_values))
+    sum_out, sum_queries, sum_values, sum_fa = total(na, nb, (part_out, part_queries, part_values, placed_fa))
+    grad_fa = lax.dynamic_slice_in_dim(sum_fa, me_b * fa_rows, fa_rows)
+    grad_fa = grad_fa.reshape(-1)[: part_fa.size].reshape(part_fa.shape)
     sum_in = jnp.concatenate([sum_queries, sum_values], axis=1)
     return (
         grad_tokens.reshape(tokens.shape),

time: 486 us -> 472 us (0.971)
  blocking collectives: 18.1 us -> 0 us
  matrix products: 40.9 us -> 46.2 us
    psum x1 -> x0, blocking collectives: 18.1 us -> none  [body(): grad_fa = lax.psum(part_fa, 'sa')]
    dot_general x3, matrix products: 12.5 us -> 18.5 us  [product_rows(): lax.dot_general(left, right, CONTRACT_ROWS, preferred_element_type=jnp.fl...]
    concatenate x1 -> x0, other arithmetic: 5.75 us -> none  [total(): jnp.concatenate([*parts, filler], axis=0)]
  transfers between devices with their start and end apart: 1 -> 1, of which waited for: 0 -> 0; matrix products, arithmetic and copies ran while one was open for 9% -> 10% of each run, Pallas kernels for 14% -> 15%
where the time goes in v3:
time: 472 us; the launch traced here: 470 us
  Pallas kernels  384 us (81%)
  matrix products  46.2 us (10%)
  other arithmetic  17.8 us (4%)
  between operations  14.2 us (3%)
  local copies, waits for them, and re-layouts  8.11 us (2%)
    pallas_call x1, Pallas kernels, mixer(): pl.pallas_call(functools.partial(mixer_kernel, dims), out_shape=(jax.Shap...  315 us
    pallas_call x1, Pallas kernels, total(): pl.pallas_call(functools.partial(total_kernel, na, nz, chunks), out_shape...  69.1 us
    dot_general x3, matrix products, product_rows(): lax.dot_general(left, right, CONTRACT_ROWS, preferred_element_type=jnp.fl...  18.5 us
    dot_general x2, matrix products, product_columns(): lax.dot_general(left, right, CONTRACT_COLUMNS, preferred_element_type=jnp...  16.4 us
  transfers between devices with their start and end apart: 1, of which 0 were waited for; matrix products, arithmetic and copies ran while one was open for 10% of the time, Pallas kernels for 15%

profile of v3, /device:TPU:0, one launch (start us, length us, event | category | flops | bytes accessed | tf_op | source)
XLA Modules:
  0.0 470.4 jit_solution(2998323572572496094)
XLA Ops:
  7.2 0.0 copy-start
  7.2 0.0 all-reduce.3.cloned.1.call-start
  7.3 7.5 %convolution_convert_fusion = bf16[2048,1536]{1,0:T(8,128)(2,1)S(1)} fusion(bf16[2048,768]{1,0:T(8,128)(2,1)} %bitcast.67, bf16[768,1536]{1,0:T(8,128)(2,1)} %param.9), kind=kOutput, calls=%fused_computation.5 | convolution fusion | flops 4834983936 | bytes 11796480 | tf_op jit(solution)/shard_map/dot_general | solution.py:528
  14.7 0.0 copy-start.1
  14.7 0.0 copy-start.6
  14.8 0.0 copy-start.7
  14.8 2.0 slice.34.v_ref
  16.8 1.5 copy-done.1
  18.3 0.0 copy-done.6
  18.4 0.0 copy-done.7
  18.4 0.1 reshape.281
  18.5 1.0 fusion.31.perm_ref
  19.5 0.0 copy-done
  19.5 10.0 %multiply_convert_fusion = (bf16[2048,768]{1,0:T(8,128)(2,1)}, f32[2048,768]{1,0:T(8,128)}) fusion(bf16[2048,1536]{1,0:T(8,128)(2,1)} %copy-done.1, bf16[2048,768]{1,0:T(8,128)(2,1)} %bitcast.65, bf16[768,768]{1,0:T(8,128)(2,1)S(1)} %copy-done), kind=kOutput, calls=%fused_computation.18 | convolution fusion | flops 2426929152 | bytes 16908288 | tf_op jit(solution)/shard_map/dot_general | solution.py:21
  29.4 0.8 fusion.30.mb_ref
  30.3 0.8 fusion.29.ma_ref
  31.1 314.8 %mixer.1 = (bf16[2048,768]{1,0:T(8,128)(2,1)}, bf16[2048,768]{1,0:T(8,128)(2,1)}, f32[4,128,128]{2,1,0:T(8,128)}, f32[256,256]{1,0:T(8,128)}, f32[256,256]{1,0:T(8,128)}) custom-call(bf16[2048,768]{1,0:T(8,128)(2,1)} %slice.34.v_ref, bf16[2048,768]{1,0:T(8,128)(2,1)} %get-tuple-element.24.g_ref, bf16[4,128,128]{2,1,0:T(8,128)(2,1)} %fc_ref.1, ...), custom_call_target="tpu_custom_call" | custom-call | tf_op jit(solution)/shard_map/mixer/pallas_call | solution.py:341
  345.9 0.0 all-reduce.3.cloned.1.call-update
  345.9 0.0 copy-start.3
  345.9 8.2 %fusion.20 = bf16[2560,768]{1,0:T(8,128)(2,1)} fusion(bf16[2048,768]{1,0:T(8,128)(2,1)} %bitcast.66, bf16[2048,768]{1,0:T(8,128)(2,1)} %get-tuple-element.11, bf16[2048,1536]{1,0:T(8,128)(2,1)} %copy-done.1), kind=kOutput, calls=%fused_computation.26 | convolution fusion | flops 2429091840 | bytes 10616832 | tf_op jit(solution)/shard_map/dot_general | solution.py:17
  354.1 0.0 copy-done.3
  354.1 0.0 copy-start.4
  354.1 6.3 %fusion.1 = bf16[2048,768]{1,0:T(8,128)(2,1)} fusion(f32[2048,768]{1,0:T(8,128)} %get-tuple-element.25, bf16[2048,768]{1,0:T(8,128)(2,1)S(1)} %copy-done.3, bf16[2048,1536]{1,0:T(8,128)(2,1)} %copy-done.1), kind=kLoop, calls=%fused_computation.7 | loop fusion | flops 18874368 | bytes 15728640 | tf_op jit(solution)/shard_map/convert_element_type | solution.py:549
  360.4 0.0 copy-done.4
  360.4 0.3 fusion.32
  360.7 0.1 reduce_sum.18
  360.8 0.1 reshape.288
  361.0 0.1 broadcast_in_dim.62
  361.1 0.1 broadcast_in_dim.63
  361.2 0.0 copy-start.8
  361.2 0.0 copy-start.9
  361.2 6.7 %fusion.24 = bf16[2560,768]{1,0:T(8,128)(2,1)} fusion(bf16[2560,768]{1,0:T(8,128)(2,1)} %fusion.20, bf16[2048,768]{1,0:T(8,128)(2,1)} %fusion.1, bf16[2048,768]{1,0:T(8,128)(2,1)} %bitcast.68), kind=kOutput, calls=%fused_computation.28 | convolution fusion | flops 2416508928 | bytes 7471104 | tf_op jit(solution)/shard_map/dot_general | solution.py:17
  367.9 0.0 copy-done.8
  367.9 0.0 copy-done.9
  367.9 3.7 fusion.26
  371.5 0.7 fusion.40
  372.2 0.8 broadcast_dynamic-update-slice_fusion
  373.0 69.1 %total.1 = bf16[2,4,4,80,768]{4,3,2,1,0:T(8,128)(2,1)S(1)} custom-call(bf16[2,4,4,80,768]{4,3,2,1,0:T(8,128)(2,1)} %bitcast.55), custom_call_target="tpu_custom_call" | custom-call | tf_op jit(solution)/shard_map/total/pallas_call | solution.py:506
  442.1 0.0 copy-start.2
  442.1 0.0 copy-start.10
  442.1 0.2 fusion.57
  442.3 1.6 convert_multiply_fusion.5
  443.9 0.6 slice.39
  444.5 0.4 copy-done.2
  444.9 0.7 copy-done.10
  445.6 6.4 %fusion.12 = bf16[2048,768]{1,0:T(8,128)(2,1)} fusion(bf16[768,1536]{1,0:T(8,128)(2,1)S(1)} %copy-done.10, bf16[2048,768]{1,0:T(8,128)(2,1)S(1)} %copy-done.9, bf16[2048,768]{1,0:T(8,128)(2,1)S(1)} %copy-done.2), kind=kOutput, calls=%fused_computation.20 | convolution fusion | flops 4845993984 | bytes 11796480 | tf_op jit(solution)/shard_map/dot_general | solution.py:21
  452.0 0.7 dynamic-slice_convert_fusion
  452.7 0.7 slice.32
  453.4 1.9 fusion.33
  455.4 1.6 reduce_sum.19
  456.9 0.9 broadcast_multiply_fusion.1
  457.8 0.6 copy.38
  458.4 0.0 copy-start.5
  458.4 2.8 convert_multiply_fusion.4
  461.3 0.0 copy-done.5
  461.3 0.6 slice_multiply_fusion
  461.9 0.0 all-reduce.3.cloned.1.call-done
  461.9 1.7 broadcast_multiply_fusion
  (13 shorter events, 0.2 us)
Async XLA Ops:
  7.2 12.3 %copy-start = (bf16[768,768]{1,0:T(8,128)(2,1)S(1)}, bf16[768,768]{1,0:T(8,128)(2,1)}, u32[]{:S(2)}) copy-start(bf16[768,768]{1,0:T(8,128)(2,1)} %param.10) | copy-start | bytes 3538948
  7.2 454.7 %all-reduce.3.cloned.1.call-start = ((), (), s32[]{:S(2)}) async-start(), calls=%async_computation | async-start | bytes 524288 | tf_op jit(solution)/shard_map/psum | solution.py:546
  14.7 3.6 copy-start.1
  14.7 3.6 copy-start.6
  14.8 3.6 copy-start.7
  345.9 8.2 %copy-start.3 = (bf16[2048,768]{1,0:T(8,128)(2,1)S(1)}, bf16[2048,768]{1,0:T(8,128)(2,1)}, u32[]{:S(2)}) copy-start(bf16[2048,768]{1,0:T(8,128)(2,1)} %get-tuple-element.11) | copy-start | bytes 9437188
  354.1 6.3 %copy-start.4 = (f32[256,256]{1,0:T(8,128)S(1)}, f32[256,256]{1,0:T(8,128)}, u32[]{:S(2)}) copy-start(f32[256,256]{1,0:T(8,128)} %get-tuple-element.13) | copy-start | bytes 786436
  361.2 6.7 %copy-start.8 = (bf16[4,4,128,768]{3,2,1,0:T(8,128)(2,1)S(1)}, bf16[4,4,128,768]{3,2,1,0:T(8,128)(2,1)}, u32[]{:S(2)}) copy-start(bf16[4,4,128,768]{3,2,1,0:T(8,128)(2,1)} %param.7) | copy-start | bytes 9437188
  361.2 6.7 %copy-start.9 = (bf16[2048,768]{1,0:T(8,128)(2,1)S(1)}, bf16[2048,768]{1,0:T(8,128)(2,1)}, u32[]{:S(2)}) copy-start(bf16[2048,768]{1,0:T(8,128)(2,1)} %get-tuple-element.12) | copy-start | bytes 9437188
  442.1 2.8 copy-start.2
  442.1 3.5 copy-start.10
  458.4 2.8 copy-start.5
Sparse Core Ops, SparseCore 0:
  346.1 60.5 all-reduce.2
